TPU v7x, 512 devices: a whole 4x4x16 slice. The times are simulated.
512 devices in a mesh: px: 32 (over x, z_lo), py: 16 (over y, z_hi, core).
Axes of the slice: x: 4, y: 4, z: 16 (z_hi: 2, z_lo: 8; z = z_hi * 8 + z_lo), core: 2. Of those that a mesh axis runs over, the one named last changes fastest.
Arguments:
- start_field: float32 [512, 512, 256], P('px', 'py'), may hold values from 0.25 to 4
- end_adjoint: float32 [512, 512, 256], P('px', 'py'), may hold values from 0.25 to 4
- potential: float32 [512, 512, 256], P('px', 'py'), may hold values from -15 to 15
- line_xy: float32 [512, 512], replicated, may hold values from -1 to 2
- line_z: float32 [256, 256], replicated, may hold values from -1 to 2
Outputs:
- final_field: float32 [512, 512, 256], P('px', 'py')
- first_adjoint: float32 [512, 512, 256], P('px', 'py')
- density: float32 [512, 512, 256], P('px', 'py')
All inputs are finite; a program needn't handle non-finite values.
Results may differ from a plain program's by a relative error of at most 0.0001.
Values sent between devices are 32-bit elements; how exact they have to be, the bound alone decides.
A program may use at most 64 MiB of HBM per device.

v0:
```python
import jax
import jax.numpy as jnp
from jax import lax
from jax.sharding import PartitionSpec as P

STEPS = 1


def product(left, right):
    return jnp.dot(left, right, precision=lax.Precision.HIGHEST, preferred_element_type=jnp.float32)


def body(start_field, end_adjoint, potential, line_xy, line_z):
    count_px = lax.axis_size("px")
    count_py = lax.axis_size("py")
    cells_x, cells_y, full_z = start_field.shape
    full_x = line_xy.shape[0]
    block_z = full_z // count_py
    block_y = full_x // count_px
    xy_turned = line_xy.T
    z_turned = line_z.T

    def sweep_last(stacked, kinds):
        pieces = [product(stacked[0], line_z if kinds[0] else z_turned)]
        return jnp.stack(pieces)

    def sweep_first(stacked, kinds):
        pieces = [product(xy_turned if kinds[0] else line_xy, stacked[0])]
        return jnp.stack(pieces)

    def z_to_y(stacked):
        fields = stacked.shape[0]
        send = stacked.reshape(fields, cells_x, cells_y, count_py, block_z).transpose(0, 2, 3, 1, 4)
        send = send.reshape(fields, cells_y, count_py * cells_x * block_z)
        return lax.all_to_all(send, "py", split_axis=2, concat_axis=1, tiled=True)

    def y_to_x(stacked):
        fields = stacked.shape[0]
        send = stacked.reshape(fields, full_x, cells_x, block_z).transpose(0, 2, 1, 3)
        send = send.reshape(fields, cells_x, full_x * block_z)
        return lax.all_to_all(send, "px", split_axis=2, concat_axis=1, tiled=True)

    def x_to_y(stacked):
        fields = stacked.shape[0]
        send = stacked.reshape(fields, full_x, block_y, block_z).transpose(0, 2, 1, 3)
        send = send.reshape(fields, block_y, full_x * block_z)
        return lax.all_to_all(send, "px", split_axis=2, concat_axis=1, tiled=True)

    def y_to_z(stacked):
        fields = stacked.shape[0]
        send = stacked.reshape(fields, count_py, cells_y, cells_x, block_z)
        got = lax.all_to_all(send, "py", split_axis=1, concat_axis=4, tiled=True)
        got = got.reshape(fields, cells_y, cells_x, count_py * block_z).transpose(0, 2, 1, 3)
        return got.reshape(fields, cells_x * cells_y, full_z)

    half_z = jnp.exp(-0.05 * potential).reshape(cells_x * cells_y, full_z)

    def contour_step(stacked, kinds):
        stacked = stacked * half_z
        stacked = sweep_last(stacked, kinds)
        stacked = z_to_y(stacked)
        stacked = sweep_first(stacked, kinds)
        stacked = y_to_x(stacked)
        stacked = sweep_first(stacked, kinds)
        stacked = y_to_z(x_to_y(stacked))
        return (stacked * half_z, "z")

    forward_list = [start_field.reshape(1, cells_x * cells_y, full_z)]
    adjoint_list = [end_adjoint.reshape(1, cells_x * cells_y, full_z)]
    layouts = ["z"]
    layout = "z"
    moved, layout = contour_step(forward_list[-1], (False,))
    forward_list.append(moved)
    layouts.append(layout)
    layout = "z"
    index = 0
    moved, layout = contour_step(adjoint_list[-1], (True,))
    adjoint_list.append(moved)
    adjoint_list = adjoint_list[::-1]
    density_z = jnp.zeros((cells_x * cells_y, full_z), jnp.float32)
    for index in range(STEPS + 1):
        weight = 0.5
        term = 0.1 * weight * forward_list[index][0] * adjoint_list[index][0]
        density_z = density_z + term
    shape = (cells_x, cells_y, full_z)
    return (
        forward_list[-1][0].reshape(shape),
        adjoint_list[0][0].reshape(shape),
        density_z.reshape(shape),
    )


def solution(mesh):
    placed = (P("px", "py", None), P("px", "py", None), P("px", "py", None), P(), P())
    return jax.shard_map(
        body,
        mesh=mesh,
        in_specs=placed,
        out_specs=(P("px", "py", None), P("px", "py", None), P("px", "py", None)),
        check_vma=False,
    )
```

profile of v0, /device:TPU:33, one launch (start us, length us, event | category | flops | bytes accessed | tf_op | source)
XLA Modules:
  0.0 516.1 jit_solution(7177278702086095888)
XLA Ops:
  0.6 3.2 convolution_bitcast_fusion.1
  3.8 1.6 copy.100
  5.9 19.1 %reduce.7 = f32[4096,32]{1,0:T(8,128)S(1)} reduce(f32[4096,1,32]{2,1,0:T(1,128)} %bitcast.138, f32[]{:T(128)} %broadcast.7), dimensions={1}, to_apply=%bitcast.88.reduce_sub_computation | reduce | bytes 1048580
  25.0 1.7 reshape.117
  26.7 17.9 %all-to-all-start = ((f32[16,1,8192]{2,1,0:T(1,128)}), f32[16,1,8192]{2,1,0:T(1,128)}, u32[]{:S(2)}, u32[]{:S(2)}) async-start(f32[16,1,8192]{2,1,0:T(1,128)} %reshape.117), calls=%async_computation | async-start | bytes 1048576 | tf_op jit(solution)/shard_map/all_to_all | solution.py:35
  44.7 3.0 convolution_bitcast_fusion
  47.7 1.6 copy.115
  49.3 19.1 %reduce = f32[4096,32]{1,0:T(8,128)S(1)} reduce(f32[4096,1,32]{2,1,0:T(1,128)} %bitcast.139, f32[]{:T(128)} %broadcast.7), dimensions={1}, to_apply=%bitcast.96.reduce_sub_computation | reduce | bytes 1048580
  68.4 1.7 reshape.125
  70.1 9.8 %all-to-all-done = f32[16,1,8192]{2,1,0:T(1,128)} async-done(((f32[16,1,8192]{2,1,0:T(1,128)}), f32[16,1,8192]{2,1,0:T(1,128)}, u32[]{:S(2)}, u32[]{:S(2)}) %all-to-all-start) | async-done | bytes 524320 | tf_op jit(solution)/shard_map/all_to_all | solution.py:35
  79.9 5.7 %all-to-all-start.4 = ((f32[16,1,8192]{2,1,0:T(1,128)}), f32[16,1,8192]{2,1,0:T(1,128)}, u32[]{:S(2)}, u32[]{:S(2)}) async-start(f32[16,1,8192]{2,1,0:T(1,128)} %reshape.125), calls=%async_computation.4 | async-start | bytes 1048576 | tf_op jit(solution)/shard_map/all_to_all | solution.py:35
  85.6 3.7 reduce.8
  89.3 4.5 reshape.118
  93.9 1.5 copy.131
  96.7 1.9 fusion.8
  98.5 2.6 copy.104
  101.2 5.8 %copy.132 = f32[1,16,512,16]{1,3,2,0:T(8,128)} copy(f32[1,16,512,16]{3,2,1,0:T(8,128)} %bitcast.124) | data formatting | bytes 1048576 | tf_op jit(solution)/shard_map/reshape | solution.py:40
  107.0 38.4 %reduce.9 = f32[8192,16]{1,0:T(8,128)} reduce(f32[8192,1,16]{2,1,0:T(1,128)} %bitcast.125, f32[]{:T(128)} %broadcast.7), dimensions={1}, to_apply=%bitcast.90.reduce_sub_computation | reduce | bytes 1048580
  145.4 4.2 reshape.119
  149.6 8.0 %all-to-all-start.1 = ((f32[32,1,4096]{2,1,0:T(1,128)}), f32[32,1,4096]{2,1,0:T(1,128)}, u32[]{:S(2)}, u32[]{:S(2)}) async-start(f32[32,1,4096]{2,1,0:T(1,128)} %reshape.119), calls=%async_computation.1 | async-start | bytes 1048576 | tf_op jit(solution)/shard_map/all_to_all | solution.py:41
  157.6 3.7 reduce.1
  161.4 4.5 reshape.126
  169.8 2.6 copy.119
  172.4 5.8 %copy.136 = f32[1,16,512,16]{1,3,2,0:T(8,128)} copy(f32[1,16,512,16]{3,2,1,0:T(8,128)} %bitcast.126) | data formatting | bytes 1048576 | tf_op jit(solution)/shard_map/reshape | solution.py:40
  178.2 38.4 %reduce.2 = f32[8192,16]{1,0:T(8,128)} reduce(f32[8192,1,16]{2,1,0:T(1,128)} %bitcast.127, f32[]{:T(128)} %broadcast.7), dimensions={1}, to_apply=%bitcast.98.reduce_sub_computation | reduce | bytes 1048580
  216.6 4.2 reshape.127
  220.8 12.3 %all-to-all-start.5 = ((f32[32,1,4096]{2,1,0:T(1,128)}), f32[32,1,4096]{2,1,0:T(1,128)S(1)}, u32[]{:S(2)}, u32[]{:S(2)}) async-start(f32[32,1,4096]{2,1,0:T(1,128)} %reshape.127), calls=%async_computation.5 | async-start | bytes 1048576 | tf_op jit(solution)/shard_map/all_to_all | solution.py:41
  233.2 2.9 reduce.10
  236.1 9.2 %reshape.120 = f32[8192,1,16]{2,1,0:T(1,128)} reshape(f32[32,4096]{1,0:T(8,128)S(1)} %reduce.10) | data formatting | bytes 1048576
  245.4 2.9 copy.133
  248.6 1.9 fusion.9
  250.5 2.6 copy.108
  253.1 5.8 %copy.134 = f32[1,16,512,16]{1,3,2,0:T(8,128)} copy(f32[1,16,512,16]{3,2,1,0:T(8,128)} %bitcast.128) | data formatting | bytes 1048576 | tf_op jit(solution)/shard_map/reshape | solution.py:46
  258.9 38.4 %reduce.11 = f32[8192,16]{1,0:T(8,128)} reduce(f32[8192,1,16]{2,1,0:T(1,128)} %bitcast.129, f32[]{:T(128)} %broadcast.7), dimensions={1}, to_apply=%bitcast.92.reduce_sub_computation | reduce | bytes 1048580
  297.3 4.4 reshape.121
  301.7 11.9 %all-to-all-start.2 = ((f32[32,1,4096]{2,1,0:T(1,128)}), f32[32,1,4096]{2,1,0:T(1,128)S(1)}, u32[]{:S(2)}, u32[]{:S(2)}) async-start(f32[32,1,4096]{2,1,0:T(1,128)} %reshape.121), calls=%async_computation.2 | async-start | bytes 1048576 | tf_op jit(solution)/shard_map/all_to_all | solution.py:47
  313.6 1.9 reduce.3
  315.5 9.2 %reshape.128 = f32[8192,1,16]{2,1,0:T(1,128)} reshape(f32[32,4096]{1,0:T(8,128)S(1)} %reduce.3) | data formatting | bytes 1048576
  324.8 2.9 copy.137
  329.0 2.6 copy.123
  331.7 5.8 %copy.138 = f32[1,16,512,16]{1,3,2,0:T(8,128)} copy(f32[1,16,512,16]{3,2,1,0:T(8,128)} %bitcast.130) | data formatting | bytes 1048576 | tf_op jit(solution)/shard_map/reshape | solution.py:46
  337.5 38.4 %reduce.4 = f32[8192,16]{1,0:T(8,128)} reduce(f32[8192,1,16]{2,1,0:T(1,128)} %bitcast.131, f32[]{:T(128)} %broadcast.7), dimensions={1}, to_apply=%bitcast.100.reduce_sub_computation | reduce | bytes 1048580
  375.9 4.2 reshape.129
  380.1 11.9 %all-to-all-start.6 = ((f32[32,1,4096]{2,1,0:T(1,128)}), f32[32,1,4096]{2,1,0:T(1,128)S(1)}, u32[]{:S(2)}, u32[]{:S(2)}) async-start(f32[32,1,4096]{2,1,0:T(1,128)} %reshape.129), calls=%async_computation.6 | async-start | bytes 1048576 | tf_op jit(solution)/shard_map/all_to_all | solution.py:47
  392.0 1.9 reduce.12
  393.9 9.2 %reshape.122 = f32[8192,1,16]{2,1,0:T(1,128)} reshape(f32[32,4096]{1,0:T(8,128)S(1)} %reduce.12) | data formatting | bytes 1048576
  403.2 2.8 copy.110
  406.0 2.6 reshape.104
  408.6 3.1 copy.111
  411.6 1.7 reshape.123
  413.4 4.8 all-to-all-done.6
  418.2 19.0 %all-to-all-start.3 = ((f32[16,1,8192]{2,1,0:T(1,128)}), f32[16,1,8192]{2,1,0:T(1,128)}, u32[]{:S(2)}, u32[]{:S(2)}) async-start(f32[16,1,8192]{2,1,0:T(1,128)} %reshape.123), calls=%async_computation.3 | async-start | bytes 1048576 | tf_op jit(solution)/shard_map/all_to_all | solution.py:52
  437.2 1.9 reduce.5
  439.1 9.2 %reshape.130 = f32[8192,1,16]{2,1,0:T(1,128)} reshape(f32[32,4096]{1,0:T(8,128)S(1)} %reduce.5) | data formatting | bytes 1048576
  448.4 2.8 copy.125
  451.1 2.6 reshape.110
  453.8 3.1 copy.126
  456.8 1.7 reshape.131
  458.5 12.3 %all-to-all-done.3 = f32[16,1,8192]{2,1,0:T(1,128)} async-done(((f32[16,1,8192]{2,1,0:T(1,128)}), f32[16,1,8192]{2,1,0:T(1,128)}, u32[]{:S(2)}, u32[]{:S(2)}) %all-to-all-start.3) | async-done | bytes 524320 | tf_op jit(solution)/shard_map/all_to_all | solution.py:52
  470.8 4.2 all-to-all-start.7
  475.0 3.0 reduce.13
  480.4 27.9 %all-to-all-done.7 = f32[16,1,8192]{2,1,0:T(1,128)S(1)} async-done(((f32[16,1,8192]{2,1,0:T(1,128)}), f32[16,1,8192]{2,1,0:T(1,128)S(1)}, u32[]{:S(2)}, u32[]{:S(2)}) %all-to-all-start.7) | async-done | bytes 524320 | tf_op jit(solution)/shard_map/all_to_all | solution.py:52
  508.3 1.9 reduce.6
  512.6 3.0 multiply_add_fusion
  (27 shorter events, 12.3 us)
Async XLA Ops:
  0.6 96.0 %copy-start = (f32[512,512]{1,0:T(8,128)S(1)}, f32[512,512]{1,0:T(8,128)}, u32[]{:S(2)}) copy-start(f32[512,512]{1,0:T(8,128)} %param.8) | copy-start | bytes 3145732
  25.0 19.6 %copy-start.2 = (f32[256,256]{1,0:T(8,128)S(1)}, f32[256,256]{1,0:T(8,128)}, u32[]{:S(2)}) copy-start(f32[256,256]{1,0:T(8,128)} %param.9) | copy-start | bytes 786436
  26.7 53.2 %all-to-all-start = ((f32[16,1,8192]{2,1,0:T(1,128)}), f32[16,1,8192]{2,1,0:T(1,128)}, u32[]{:S(2)}, u32[]{:S(2)}) async-start(f32[16,1,8192]{2,1,0:T(1,128)} %reshape.117), calls=%async_computation | async-start | bytes 1048576 | tf_op jit(solution)/shard_map/all_to_all | solution.py:35
  79.9 69.7 %all-to-all-start.4 = ((f32[16,1,8192]{2,1,0:T(1,128)}), f32[16,1,8192]{2,1,0:T(1,128)}, u32[]{:S(2)}, u32[]{:S(2)}) async-start(f32[16,1,8192]{2,1,0:T(1,128)} %reshape.125), calls=%async_computation.4 | async-start | bytes 1048576 | tf_op jit(solution)/shard_map/all_to_all | solution.py:35
  149.6 71.3 %all-to-all-start.1 = ((f32[32,1,4096]{2,1,0:T(1,128)}), f32[32,1,4096]{2,1,0:T(1,128)}, u32[]{:S(2)}, u32[]{:S(2)}) async-start(f32[32,1,4096]{2,1,0:T(1,128)} %reshape.119), calls=%async_computation.1 | async-start | bytes 1048576 | tf_op jit(solution)/shard_map/all_to_all | solution.py:41
  220.8 80.8 %all-to-all-start.5 = ((f32[32,1,4096]{2,1,0:T(1,128)}), f32[32,1,4096]{2,1,0:T(1,128)S(1)}, u32[]{:S(2)}, u32[]{:S(2)}) async-start(f32[32,1,4096]{2,1,0:T(1,128)} %reshape.127), calls=%async_computation.5 | async-start | bytes 1048576 | tf_op jit(solution)/shard_map/all_to_all | solution.py:41
  301.7 78.4 %all-to-all-start.2 = ((f32[32,1,4096]{2,1,0:T(1,128)}), f32[32,1,4096]{2,1,0:T(1,128)S(1)}, u32[]{:S(2)}, u32[]{:S(2)}) async-start(f32[32,1,4096]{2,1,0:T(1,128)} %reshape.121), calls=%async_computation.2 | async-start | bytes 1048576 | tf_op jit(solution)/shard_map/all_to_all | solution.py:47
  380.1 38.1 %all-to-all-start.6 = ((f32[32,1,4096]{2,1,0:T(1,128)}), f32[32,1,4096]{2,1,0:T(1,128)S(1)}, u32[]{:S(2)}, u32[]{:S(2)}) async-start(f32[32,1,4096]{2,1,0:T(1,128)} %reshape.129), calls=%async_computation.6 | async-start | bytes 1048576 | tf_op jit(solution)/shard_map/all_to_all | solution.py:47
  418.2 52.7 %all-to-all-start.3 = ((f32[16,1,8192]{2,1,0:T(1,128)}), f32[16,1,8192]{2,1,0:T(1,128)}, u32[]{:S(2)}, u32[]{:S(2)}) async-start(f32[16,1,8192]{2,1,0:T(1,128)} %reshape.123), calls=%async_computation.3 | async-start | bytes 1048576 | tf_op jit(solution)/shard_map/all_to_all | solution.py:52
  470.8 37.5 %all-to-all-start.7 = ((f32[16,1,8192]{2,1,0:T(1,128)}), f32[16,1,8192]{2,1,0:T(1,128)S(1)}, u32[]{:S(2)}, u32[]{:S(2)}) async-start(f32[16,1,8192]{2,1,0:T(1,128)} %reshape.131), calls=%async_computation.7 | async-start | bytes 1048576 | tf_op jit(solution)/shard_map/all_to_all | solution.py:52
  511.3 4.4 copy-start.1
where the time goes:
time: 524 us; the launch traced here: 516 us
  other arithmetic  216 us (41%)
  local copies, waits for them, and re-layouts  141 us (27%)
  starting transfers between devices  91 us (17%)
  waiting for transfers between devices  54.8 us (10%)
  matrix products  12.1 us (2%)
    unnamed x6, other arithmetic  192 us
    unnamed x24, local copies, waits for them, and re-layouts  71.9 us
    all_to_all x2, waiting for transfers between devices, y_to_z(): got = lax.all_to_all(send, 'py', split_axis=1, concat_axis=4, tiled=True)  40.2 us
    all_to_all x2, starting transfers between devices, x_to_y(): return lax.all_to_all(send, 'px', split_axis=2, concat_axis=1, tiled=True)  23.9 us
    all_to_all x2, starting transfers between devices, z_to_y(): return lax.all_to_all(send, 'py', split_axis=2, concat_axis=1, tiled=True)  23.5 us
    all_to_all x2, starting transfers between devices, y_to_z(): got = lax.all_to_all(send, 'py', split_axis=1, concat_axis=4, tiled=True)  23.2 us
    all_to_all x2, starting transfers between devices, y_to_x(): return lax.all_to_all(send, 'px', split_axis=2, concat_axis=1, tiled=True)  20.4 us
    dot_general x6, matrix products, product(): jnp.dot(left, right, precision=lax.Precision.HIGHEST, preferred_element_t...  12.1 us
  transfers between devices with their start and end apart: 8, of which 4 were waited for; matrix products, arithmetic and copies ran while one was open for 65% of the time, Pallas kernels for 0%

commit v1 on v0

v1 whole, which is shorter than its diff:
```python
import functools
import jax
import jax.numpy as jnp
from jax import lax
from jax.sharding import PartitionSpec as P
from jax.experimental import pallas as pl
from jax.experimental.pallas import tpu as pltpu

MESH = pl.DeviceIdType.MESH
F32 = jnp.float32
BF16 = jnp.bfloat16
NX_CHIPS, NY_CHIPS, NZ_CHIPS = 4, 4, 16


def split(value):
    high = value.astype(BF16)
    return high, (value - high.astype(F32)).astype(BF16)


def contract(left, right, dims):
    return lax.dot_general(left, right, (dims, ((), ())), preferred_element_type=F32)


NN = ((1,), (0,))
NT = ((1,), (1,))


def contract3(left, right, dims):
    (left_high, left_low), (right_high, right_low) = left, right
    return contract(left_high, right_high, dims) + (
        contract(left_high, right_low, dims) + contract(left_low, right_high, dims)
    )


def kernel(
    start_hbm, end_hbm, potential_hbm, xy_hbm, z_hbm,
    final_hbm, first_hbm, density_hbm,
    field, half, pot, xy, lz, result,
    send_z, got_z, gather_x, gather_y, part_send, part_got, part_own, send_back, got_back,
    weight_x, weight_y,
    in_sem, out_sem, z_send_sem, z_recv_sem, x_send_sem, x_recv_sem, y_send_sem, y_recv_sem,
    c_send_sem, c_recv_sem, b_send_sem, b_recv_sem,
):
    px, py = lax.axis_index("px"), lax.axis_index("py")
    x, z_low = px // 8, px % 8
    y, z_high, core = py // 4, (py // 2) % 2, py % 2
    z = z_high * 8 + z_low

    def device(x_at, y_at, z_at, core_at):
        return {"px": x_at * 8 + z_at % 8, "py": y_at * 4 + (z_at // 8) * 2 + core_at}

    loads = [
        pltpu.make_async_copy(source, target, in_sem.at[i])
        for i, (source, target) in enumerate(
            [(potential_hbm, pot), (start_hbm, field.at[0]), (z_hbm, lz), (xy_hbm, xy), (end_hbm, field.at[1])]
        )
    ]
    for load in loads:
        load.start()
    barrier = pltpu.get_barrier_semaphore()

    def signal(target):
        pl.semaphore_signal(barrier, inc=1, device_id=target, device_id_type=MESH)

    @pl.loop(1, NZ_CHIPS)
    def _(step):
        signal(device(x, y, (z + step) % NZ_CHIPS, core))

    for step in range(1, 4):
        signal(device((x + step) % 4, y, z, core))
        signal(device(x, (y + step) % 4, z, core))
    signal(device(x, y, z, 1 - core))

    def exchange_z(source, target, send_sem, recv_sem, chunk):
        @pl.loop(1, NZ_CHIPS)
        def _(step):
            peer = (z + step) % NZ_CHIPS
            pltpu.make_async_remote_copy(
                source.at[chunk, pl.ds(pl.multiple_of(peer * 32, 32), 32)],
                target.at[chunk, pl.ds(pl.multiple_of(z * 32, 32), 32)],
                send_sem.at[chunk], recv_sem.at[chunk],
                device_id=device(x, y, peer, core), device_id_type=MESH,
            ).start()

        mine = pl.ds(pl.multiple_of(z * 32, 32), 32)
        pltpu.make_async_copy(source.at[chunk, mine], target.at[chunk, mine], recv_sem.at[chunk]).start()

    def wait_z(target, recv_sem, chunk):
        pltpu.make_async_copy(target.at[chunk], target.at[chunk], recv_sem.at[chunk]).wait()

    def wait_z_sent(source, send_sem, chunk):
        sent = source.at[chunk, pl.ds(0, 480)]
        pltpu.make_async_copy(sent, sent, send_sem.at[chunk]).wait()

    def ring_copies(buffer, send_sem, recv_sem, chunk, axis):
        here = x if axis == 0 else y
        copies = []
        for step in (1, 3, 2):
            there = (here + step) % 4
            target = device(there, y, z, core) if axis == 0 else device(x, there, z, core)
            copies.append(
                pltpu.make_async_remote_copy(
                    buffer.at[chunk, here], buffer.at[chunk, here],
                    send_sem.at[chunk, step - 1], recv_sem.at[chunk, step - 1],
                    device_id=target, device_id_type=MESH,
                )
            )
        return copies

    def core_copy(chunk):
        return pltpu.make_async_remote_copy(
            part_send.at[chunk], part_got.at[chunk], c_send_sem.at[chunk], c_recv_sem.at[chunk],
            device_id=device(x, y, z, 1 - core), device_id_type=MESH,
        )

    lane = lax.broadcasted_iota(jnp.int32, (8, 128), 1)
    low_64 = lane % 128 < 64
    low_32 = lane % 64 < 32

    def regroup(a, b, c, d):
        a, c = jnp.where(low_64, a, pltpu.roll(c, 64, 1)), jnp.where(low_64, pltpu.roll(a, 64, 1), c)
        b, d = jnp.where(low_64, b, pltpu.roll(d, 64, 1)), jnp.where(low_64, pltpu.roll(b, 64, 1), d)
        a, b = jnp.where(low_32, a, pltpu.roll(b, 32, 1)), jnp.where(low_32, pltpu.roll(a, 96, 1), b)
        c, d = jnp.where(low_32, c, pltpu.roll(d, 32, 1)), jnp.where(low_32, pltpu.roll(c, 96, 1), d)
        return a, b, c, d

    def step_z(chunk, line, values):
        value = contract3(line, values, NT)
        for at in range(16):
            for tile in range(4):
                send_z[chunk, pl.ds(at * 32 + tile * 8, 8)] = value[at * 8 : at * 8 + 8, tile * 128 : tile * 128 + 128]

    def step_z_send(chunk):
        exchange_z(send_z, got_z, z_send_sem, z_recv_sem, chunk)

    def step_x_send(chunk):
        wait_z(got_z, z_recv_sem, chunk)
        for pair in range(4):
            for tile in range(4):
                parts = [
                    got_z[chunk, pl.ds(high * 256 + tile * 8 + pair * 2 + p, 8, stride=32), :]
                    for p in range(2) for high in range(2)
                ]
                for i, part in enumerate(regroup(*parts)):
                    gather_x[chunk, x, pl.ds((tile * 4 + i) * 8, 8), pl.ds(pair * 128, 128)] = part
        for copy in ring_copies(gather_x, x_send_sem, x_recv_sem, chunk, 0):
            copy.start()

    def step_y_send(chunk):
        kind = chunk // 2
        for copy in ring_copies(gather_x, x_send_sem, x_recv_sem, chunk, 0):
            copy.wait_recv()
        values = split(gather_x[chunk].reshape(512, 512))
        gather_y[chunk, y] = contract3((weight_x[kind, 0], weight_x[kind, 1]), values, NN)
        for copy in ring_copies(gather_y, y_send_sem, y_recv_sem, chunk, 1):
            copy.start()

    def step_core_send(chunk):
        kind = chunk // 2
        for copy in ring_copies(gather_y, y_send_sem, y_recv_sem, chunk, 1):
            copy.wait_recv()
        weights = (weight_y[kind, 0], weight_y[kind, 1])
        for pair in range(4):
            lanes = pl.ds(pair * 128, 128)
            values = jnp.concatenate([gather_y[chunk, k, :, lanes] for k in range(4)], axis=1)
            out = contract3(split(values), weights, NN)
            part_own[chunk, :, lanes] = out[:, :128]
            part_send[chunk, :, lanes] = out[:, 128:]
        core_copy(chunk).start()

    def step_back(chunk):
        core_copy(chunk).wait_recv()
        for pair in range(4):
            for tile in range(4):
                parts = []
                for i in range(4):
                    at = (chunk, pl.ds((tile * 4 + i) * 8, 8), pl.ds(pair * 128, 128))
                    parts.append(part_own[at] + part_got[at])
                parts = regroup(*parts)
                for p in range(2):
                    for high in range(2):
                        rows = pl.ds(high * 256 + tile * 8 + pair * 2 + p, 8, stride=32)
                        send_back[chunk, rows, :] = parts[p * 2 + high]
        exchange_z(send_back, got_back, b_send_sem, b_recv_sem, chunk)

    def out_copy(chunk, slot, target):
        lanes = pl.ds((chunk % 2) * 128, 128)
        return pltpu.make_async_copy(
            result.at[slot, :, :, lanes], target.at[:, :, lanes], out_sem.at[slot, chunk % 2]
        )

    def step_last(chunk):
        kind = chunk // 2
        lanes = pl.ds((chunk % 2) * 128, 128)
        wait_z(got_back, b_recv_sem, chunk)
        arrived = got_back[chunk].reshape(16, 4, 8, 128)
        value = jnp.concatenate(
            [jnp.transpose(arrived[:, tile].reshape(128, 128)).reshape(4, 32, 128) for tile in range(4)]
        ) * half[:, :, lanes]
        result[kind, :, :, lanes] = value
        if kind == 0:
            out_copy(chunk, 0, final_hbm).start()
        else:
            out_copy(chunk, 1, first_hbm).start()
            result[2, :, :, lanes] = 0.05 * (
                field[0, :, :, lanes] * value + result[0, :, :, lanes] * field[1, :, :, lanes]
            )
            out_copy(chunk, 2, density_hbm).start()

    loads[0].wait()
    loads[1].wait()
    half[...] = jnp.exp(-0.05 * pot[...])
    values = split((half[...] * field[0]).reshape(512, 256))
    loads[2].wait()
    step_z(0, split(lz[:128, :]), values)
    pl.semaphore_wait(barrier, 22)
    step_z_send(0)
    step_z(1, split(lz[128:, :]), values)
    step_z_send(1)

    loads[3].wait()
    loads[4].wait()
    row = lax.broadcasted_iota(jnp.int32, (128, 128), 0)
    column = lax.broadcasted_iota(jnp.int32, (128, 128), 1)
    order_x = (column == (row % 8) * 16 + row // 8).astype(F32).astype(BF16)
    order_y = (column == (row % 64) // 32 * 64 + core * 32 + row % 32).astype(F32).astype(BF16)
    row = lax.broadcasted_iota(jnp.int32, (256, 128), 0)
    column = lax.broadcasted_iota(jnp.int32, (256, 128), 1)
    other = (core + row // 128) % 2
    order_out = (column == (row % 64) // 32 * 64 + other * 32 + row % 32).astype(F32).astype(BF16)
    row = lax.broadcasted_iota(jnp.int32, (128, 256), 0)
    column = lax.broadcasted_iota(jnp.int32, (128, 256), 1)
    same = row // 64 == column % 128 // 64
    at_x = pl.ds(pl.multiple_of(x * 128, 128), 128)
    at_y = pl.ds(pl.multiple_of(y * 128, 128), 128)
    for kind in range(2):
        for k in range(4):
            block = pl.ds(k * 128, 128)
            if kind == 0:
                of_x, of_y = split(xy[at_x, block]), split(xy[at_y, block])
            else:
                of_x, of_y = split(xy[block, at_x]), split(xy[block, at_y])
            for part in range(2):
                turned = contract(order_x, of_x[part], NN if kind == 0 else NT).astype(BF16)
                weight_x[kind, part, :, block] = contract(turned, order_x, NT).astype(BF16)
                turned = contract(order_y, of_y[part], NT if kind == 0 else NN).astype(BF16)
                weight_y[kind, part, block, :] = jnp.where(same, contract(turned, order_out, NT), 0.0).astype(BF16)

    turned = jnp.transpose(lz[...])
    values = split((half[...] * field[1]).reshape(512, 256))
    step_z(2, split(turned[:128, :]), values)
    step_z(3, split(turned[128:, :]), values)

    step_x_send(0)
    step_z_send(2)
    step_x_send(1)
    step_z_send(3)
    step_y_send(0)
    step_x_send(2)
    step_y_send(1)
    step_core_send(0)
    step_x_send(3)
    step_back(0)
    step_y_send(2)
    step_core_send(1)
    step_back(1)
    step_y_send(3)
    step_core_send(2)
    step_back(2)
    step_core_send(3)
    step_back(3)
    for chunk in range(4):
        step_last(chunk)

    for chunk in range(4):
        wait_z_sent(send_z, z_send_sem, chunk)
        wait_z_sent(send_back, b_send_sem, chunk)
        for copy in ring_copies(gather_x, x_send_sem, x_recv_sem, chunk, 0):
            copy.wait_send()
        for copy in ring_copies(gather_y, y_send_sem, y_recv_sem, chunk, 1):
            copy.wait_send()
        core_copy(chunk).wait_send()
    for half_z in range(2):
        out_copy(half_z, 0, final_hbm).wait()
        out_copy(half_z, 1, first_hbm).wait()
        out_copy(half_z, 2, density_hbm).wait()


def body(start_field, end_adjoint, potential, line_xy, line_z):
    shape = start_field.shape
    dma = pltpu.SemaphoreType.DMA
    chunk = (4, 128, 512)
    pieces = (4, 512, 128)
    gather = (4, 4, 128, 512)
    return pl.pallas_call(
        kernel,
        out_shape=[jax.ShapeDtypeStruct(shape, F32)] * 3,
        in_specs=[pl.BlockSpec(memory_space=pl.ANY)] * 5,
        out_specs=[pl.BlockSpec(memory_space=pl.ANY)] * 3,
        scratch_shapes=[
            pltpu.VMEM((2,) + shape, F32),
            pltpu.VMEM(shape, F32),
            pltpu.VMEM(shape, F32),
            pltpu.VMEM(line_xy.shape, F32),
            pltpu.VMEM(line_z.shape, F32),
            pltpu.VMEM((3,) + shape, F32),
            pltpu.VMEM(pieces, F32),
            pltpu.VMEM(pieces, F32),
            pltpu.VMEM(gather, F32),
            pltpu.VMEM(gather, F32),
            pltpu.VMEM(chunk, F32),
            pltpu.VMEM(chunk, F32),
            pltpu.VMEM(chunk, F32),
            pltpu.VMEM(pieces, F32),
            pltpu.VMEM(pieces, F32),
            pltpu.VMEM((2, 2, 128, 512), BF16),
            pltpu.VMEM((2, 2, 512, 256), BF16),
            dma((5,)), dma((3, 2)), dma((4,)), dma((4,)), dma((4, 3)), dma((4, 3)), dma((4, 3)), dma((4, 3)),
            dma((4,)), dma((4,)), dma((4,)), dma((4,)),
        ],
        compiler_params=pltpu.CompilerParams(
            collective_id=0, has_side_effects=True, vmem_limit_bytes=48 * 2**20
        ),
        name="contour_step",
    )(start_field, end_adjoint, potential, line_xy, line_z)


def solution(mesh):
    placed = (P("px", "py", None), P("px", "py", None), P("px", "py", None), P(), P())
    return jax.shard_map(
        body,
        mesh=mesh,
        in_specs=placed,
        out_specs=(P("px", "py", None), P("px", "py", None), P("px", "py", None)),
        check_vma=False,
    )
```

time: 524 us -> 125 us (0.24)
  the two profiles are of different devices: /device:TPU:33 before, /device:TPU:5 now
where the time goes in v1:
time: 125 us
  Pallas kernels  117 us (94%)
  local copies, waits for them, and re-layouts  7.67 us (6%)
    pallas_call x1, Pallas kernels, body(): pl.pallas_call(kernel, out_shape=[jax.ShapeDtypeStruct(shape, F32)] * 3,...  117 us
    unnamed x13, local copies, waits for them, and re-layouts  7.67 us

profile of v1, /device:TPU:5, one launch (start us, length us, event | category | flops | bytes accessed | tf_op | source)
XLA Modules:
  0.0 124.9 jit_solution(15241697834604391669)
XLA Ops:
  0.6 0.0 copy-start
  0.6 1.2 copy-done
  1.9 0.0 copy-start.1
  1.9 1.0 copy-done.1
  2.9 0.0 copy-start.2
  2.9 1.0 copy-done.2
  3.9 0.0 copy-start.3
  3.9 1.0 copy-done.3
  5.0 0.0 copy-start.4
  5.0 0.9 copy-done.4
  5.9 116.6 %contour_step.1 = (f32[16,32,256]{2,1,0:T(8,128)S(1)}, f32[16,32,256]{2,1,0:T(8,128)S(1)}, f32[16,32,256]{2,1,0:T(8,128)S(1)}) custom-call(f32[16,32,256]{2,1,0:T(8,128)S(1)} %copy-done.1, f32[16,32,256]{2,1,0:T(8,128)S(1)} %copy-done.2, f32[16,32,256]{2,1,0:T(8,128)S(1)} %copy-done.3, f32[512,512]{1,0:T(8,128)S(1)} %copy-done, f32[256,256]{1,0:T(8,128)S(1)} %copy-done.4), custom_call_target="tpu_custom_call" | custom-call | tf_op jit(solution)/shard_map/contour_step/pallas_call | solution.py:295
  122.5 0.8 copy.11
  123.3 0.8 copy.12
  124.1 0.8 copy.13
Async XLA Ops:
  0.6 1.2 copy-start
  1.9 1.0 copy-start.1
  2.9 1.0 copy-start.2
  3.9 1.0 copy-start.3
  5.0 0.9 copy-start.4

commit v2 on v1

--- a/solution.py
+++ b/solution.py
@@ -34,11 +34,11 @@
 
 def kernel(
     start_hbm, end_hbm, potential_hbm, xy_hbm, z_hbm,
-    final_hbm, first_hbm, density_hbm,
-    field, half, pot, xy, lz, result,
+    final_out, first_out, density_out,
+    field, half, pot, xy, lz,
     send_z, got_z, gather_x, gather_y, part_send, part_got, part_own, send_back, got_back,
     weight_x, weight_y,
-    in_sem, out_sem, z_send_sem, z_recv_sem, x_send_sem, x_recv_sem, y_send_sem, y_recv_sem,
+    in_sem, z_send_sem, z_recv_sem, x_send_sem, x_recv_sem, y_send_sem, y_recv_sem,
     c_send_sem, c_recv_sem, b_send_sem, b_recv_sem,
 ):
     px, py = lax.axis_index("px"), lax.axis_index("py")
@@ -183,12 +183,6 @@
                         send_back[chunk, rows, :] = parts[p * 2 + high]
         exchange_z(send_back, got_back, b_send_sem, b_recv_sem, chunk)
 
-    def out_copy(chunk, slot, target):
-        lanes = pl.ds((chunk % 2) * 128, 128)
-        return pltpu.make_async_copy(
-            result.at[slot, :, :, lanes], target.at[:, :, lanes], out_sem.at[slot, chunk % 2]
-        )
-
     def step_last(chunk):
         kind = chunk // 2
         lanes = pl.ds((chunk % 2) * 128, 128)
@@ -197,15 +191,13 @@
         value = jnp.concatenate(
             [jnp.transpose(arrived[:, tile].reshape(128, 128)).reshape(4, 32, 128) for tile in range(4)]
         ) * half[:, :, lanes]
-        result[kind, :, :, lanes] = value
         if kind == 0:
-            out_copy(chunk, 0, final_hbm).start()
+            final_out[:, :, lanes] = value
         else:
-            out_copy(chunk, 1, first_hbm).start()
-            result[2, :, :, lanes] = 0.05 * (
-                field[0, :, :, lanes] * value + result[0, :, :, lanes] * field[1, :, :, lanes]
+            first_out[:, :, lanes] = value
+            density_out[:, :, lanes] = 0.05 * (
+                field[0, :, :, lanes] * value + final_out[:, :, lanes] * field[1, :, :, lanes]
             )
-            out_copy(chunk, 2, density_hbm).start()
 
     loads[0].wait()
     loads[1].wait()
@@ -280,10 +272,19 @@
         for copy in ring_copies(gather_y, y_send_sem, y_recv_sem, chunk, 1):
             copy.wait_send()
         core_copy(chunk).wait_send()
-    for half_z in range(2):
-        out_copy(half_z, 0, final_hbm).wait()
-        out_copy(half_z, 1, first_hbm).wait()
-        out_copy(half_z, 2, density_hbm).wait()
+
+
+def store(*refs):
+    sources, targets, sem = refs[:3], refs[3:6], refs[6]
+    copies = [pltpu.make_async_copy(a, b, sem.at[i]) for i, (a, b) in enumerate(zip(sources, targets))]
+    for copy in copies:
+        copy.start()
+    for copy in copies:
+        copy.wait()
+
+
+def in_hbm(array):
+    return pltpu.with_memory_space_constraint(array, pltpu.HBM)
 
 
 def body(start_field, end_adjoint, potential, line_xy, line_z):
@@ -292,18 +293,17 @@
     chunk = (4, 128, 512)
     pieces = (4, 512, 128)
     gather = (4, 4, 128, 512)
-    return pl.pallas_call(
+    outs = pl.pallas_call(
         kernel,
         out_shape=[jax.ShapeDtypeStruct(shape, F32)] * 3,
         in_specs=[pl.BlockSpec(memory_space=pl.ANY)] * 5,
-        out_specs=[pl.BlockSpec(memory_space=pl.ANY)] * 3,
+        out_specs=[pl.BlockSpec(memory_space=pltpu.VMEM)] * 3,
         scratch_shapes=[
             pltpu.VMEM((2,) + shape, F32),
             pltpu.VMEM(shape, F32),
             pltpu.VMEM(shape, F32),
             pltpu.VMEM(line_xy.shape, F32),
             pltpu.VMEM(line_z.shape, F32),
-            pltpu.VMEM((3,) + shape, F32),
             pltpu.VMEM(pieces, F32),
             pltpu.VMEM(pieces, F32),
             pltpu.VMEM(gather, F32),
@@ -315,14 +315,23 @@
             pltpu.VMEM(pieces, F32),
             pltpu.VMEM((2, 2, 128, 512), BF16),
             pltpu.VMEM((2, 2, 512, 256), BF16),
-            dma((5,)), dma((3, 2)), dma((4,)), dma((4,)), dma((4, 3)), dma((4, 3)), dma((4, 3)), dma((4, 3)),
+            dma((5,)), dma((4,)), dma((4,)), dma((4, 3)), dma((4, 3)), dma((4, 3)), dma((4, 3)),
             dma((4,)), dma((4,)), dma((4,)), dma((4,)),
         ],
         compiler_params=pltpu.CompilerParams(
             collective_id=0, has_side_effects=True, vmem_limit_bytes=48 * 2**20
         ),
         name="contour_step",
-    )(start_field, end_adjoint, potential, line_xy, line_z)
+    )(in_hbm(start_field), in_hbm(end_adjoint), in_hbm(potential), in_hbm(line_xy), in_hbm(line_z))
+    return pl.pallas_call(
+        store,
+        out_shape=[jax.ShapeDtypeStruct(shape, F32)] * 3,
+        in_specs=[pl.BlockSpec(memory_space=pl.ANY)] * 3,
+        out_specs=[pl.BlockSpec(memory_space=pl.ANY)] * 3,
+        scratch_shapes=[dma((3,))],
+        compiler_params=pltpu.CompilerParams(vmem_limit_bytes=8 * 2**20),
+        name="store",
+    )(*[pltpu.with_memory_space_constraint(out, pltpu.VMEM) for out in outs])
 
 
 def solution(mesh):

time: 125 us -> 118 us (0.944)
  local copies, waits for them, and re-layouts: 7.67 us -> 0 us
    unnamed x13 -> x0, local copies, waits for them, and re-layouts: 7.67 us -> none
where the time goes in v2:
time: 118 us
  Pallas kernels  117 us (99%)
    pallas_call x1, Pallas kernels, body(): pl.pallas_call(kernel, out_shape=[jax.ShapeDtypeStruct(shape, F32)] * 3,...  116 us

profile of v2, /device:TPU:5, one launch (start us, length us, event | category | flops | bytes accessed | tf_op | source)
XLA Modules:
  0.0 118.1 jit_solution(13661534020423646430)
XLA Ops:
  0.6 116.3 %contour_step.1 = (f32[16,32,256]{2,1,0:T(8,128)S(1)}, f32[16,32,256]{2,1,0:T(8,128)S(1)}, f32[16,32,256]{2,1,0:T(8,128)S(1)}) custom-call(f32[16,32,256]{2,1,0:T(8,128)} %start_hbm.1, f32[16,32,256]{2,1,0:T(8,128)} %end_hbm.1, f32[16,32,256]{2,1,0:T(8,128)} %potential_hbm.1, f32[512,512]{1,0:T(8,128)} %xy_hbm.1, f32[256,256]{1,0:T(8,128)} %z_hbm.1), custom_call_target="tpu_custom_call" | custom-call | tf_op jit(solution)/shard_map/contour_step/pallas_call | solution.py:296
  116.9 1.2 store.1

commit v3 on v2

--- a/solution.py
+++ b/solution.py
@@ -25,20 +25,24 @@
 NT = ((1,), (1,))
 
 
-def contract3(left, right, dims):
-    (left_high, left_low), (right_high, right_low) = left, right
-    return contract(left_high, right_high, dims) + (
-        contract(left_high, right_low, dims) + contract(left_low, right_high, dims)
-    )
+def stacked(value):
+    return jnp.concatenate(split(value), axis=0)
+
+
+def contract_left(left, right, dims):
+    rows = left.shape[0] // 2
+    high, low = split(right)
+    both = contract(left, high, dims)
+    return both[:rows] + (both[rows:] + contract(left[:rows], low, dims))
 
 
 def kernel(
     start_hbm, end_hbm, potential_hbm, xy_hbm, z_hbm,
     final_out, first_out, density_out,
     field, half, pot, xy, lz,
-    send_z, got_z, gather_x, gather_y, part_send, part_got, part_own, send_back, got_back,
+    send_z, got_z, out_x, in_x, turn_x, home_x, in_y, part_own, part_send, part_got, turn_y, home_y, send_back, got_back,
     weight_x, weight_y,
-    in_sem, z_send_sem, z_recv_sem, x_send_sem, x_recv_sem, y_send_sem, y_recv_sem,
+    in_sem, z_send_sem, z_recv_sem, ring_send_sem, ring_recv_sem,
     c_send_sem, c_recv_sem, b_send_sem, b_recv_sem,
 ):
     px, py = lax.axis_index("px"), lax.axis_index("py")
@@ -72,8 +76,9 @@
     signal(device(x, y, z, 1 - core))
 
     def exchange_z(source, target, send_sem, recv_sem, chunk):
-        @pl.loop(1, NZ_CHIPS)
-        def _(step):
+        @pl.loop(0, NZ_CHIPS - 1)
+        def _(i):
+            step = NZ_CHIPS // 2 + i // 2 - (i % 2) * (2 * (i // 2) + 1)
             peer = (z + step) % NZ_CHIPS
             pltpu.make_async_remote_copy(
                 source.at[chunk, pl.ds(pl.multiple_of(peer * 32, 32), 32)],
@@ -92,20 +97,34 @@
         sent = source.at[chunk, pl.ds(0, 480)]
         pltpu.make_async_copy(sent, sent, send_sem.at[chunk]).wait()
 
-    def ring_copies(buffer, send_sem, recv_sem, chunk, axis):
+    exchanges = ((out_x, in_x, 0), (turn_x, home_x, 0), (home_x, in_y, 1), (turn_y, home_y, 1))
+
+    def ring_copies(stage, chunk):
+        source, target, axis = exchanges[stage]
         here = x if axis == 0 else y
         copies = []
-        for step in (1, 3, 2):
+        for step in (2, 1, 3):
             there = (here + step) % 4
-            target = device(there, y, z, core) if axis == 0 else device(x, there, z, core)
+            peer = device(there, y, z, core) if axis == 0 else device(x, there, z, core)
             copies.append(
                 pltpu.make_async_remote_copy(
-                    buffer.at[chunk, here], buffer.at[chunk, here],
-                    send_sem.at[chunk, step - 1], recv_sem.at[chunk, step - 1],
-                    device_id=target, device_id_type=MESH,
+                    source.at[chunk, there], target.at[chunk, here],
+                    ring_send_sem.at[stage, chunk, step - 1], ring_recv_sem.at[stage, chunk, step - 1],
+                    device_id=peer, device_id_type=MESH,
                 )
             )
         return copies
+
+    def ring_start(stage, chunk):
+        source, target, axis = exchanges[stage]
+        here = x if axis == 0 else y
+        for copy in ring_copies(stage, chunk):
+            copy.start()
+        target[chunk, here] = source[chunk, here]
+
+    def ring_wait(stage, chunk):
+        for copy in ring_copies(stage, chunk):
+            copy.wait_recv()
 
     def core_copy(chunk):
         return pltpu.make_async_remote_copy(
@@ -124,8 +143,9 @@
         c, d = jnp.where(low_32, c, pltpu.roll(d, 32, 1)), jnp.where(low_32, pltpu.roll(c, 96, 1), d)
         return a, b, c, d
 
-    def step_z(chunk, line, values):
-        value = contract3(line, values, NT)
+    def step_z(chunk, line, field_values):
+        value = contract(line, field_values[0], NT)
+        value = value[:128] + (value[128:] + contract(line[:128], field_values[1], NT))
         for at in range(16):
             for tile in range(4):
                 send_z[chunk, pl.ds(at * 32 + tile * 8, 8)] = value[at * 8 : at * 8 + 8, tile * 128 : tile * 128 + 128]
@@ -133,7 +153,7 @@
     def step_z_send(chunk):
         exchange_z(send_z, got_z, z_send_sem, z_recv_sem, chunk)
 
-    def step_x_send(chunk):
+    def step_a(chunk):
         wait_z(got_z, z_recv_sem, chunk)
         for pair in range(4):
             for tile in range(4):
@@ -142,41 +162,41 @@
                     for p in range(2) for high in range(2)
                 ]
                 for i, part in enumerate(regroup(*parts)):
-                    gather_x[chunk, x, pl.ds((tile * 4 + i) * 8, 8), pl.ds(pair * 128, 128)] = part
-        for copy in ring_copies(gather_x, x_send_sem, x_recv_sem, chunk, 0):
-            copy.start()
-
-    def step_y_send(chunk):
+                    out_x[chunk, pair, pl.ds((tile * 4 + i) * 8, 8), :] = part
+        ring_start(0, chunk)
+
+    def step_b(chunk):
+        ring_wait(0, chunk)
+        values = in_x[chunk].reshape(512, 128)
+        turn_x[chunk] = contract_left(weight_x[chunk // 2], values, NN).reshape(4, 128, 128)
+        ring_start(1, chunk)
+
+    def step_c(chunk):
+        ring_wait(1, chunk)
+        ring_start(2, chunk)
+
+    def step_d(chunk):
         kind = chunk // 2
-        for copy in ring_copies(gather_x, x_send_sem, x_recv_sem, chunk, 0):
-            copy.wait_recv()
-        values = split(gather_x[chunk].reshape(512, 512))
-        gather_y[chunk, y] = contract3((weight_x[kind, 0], weight_x[kind, 1]), values, NN)
-        for copy in ring_copies(gather_y, y_send_sem, y_recv_sem, chunk, 1):
-            copy.start()
-
-    def step_core_send(chunk):
-        kind = chunk // 2
-        for copy in ring_copies(gather_y, y_send_sem, y_recv_sem, chunk, 1):
-            copy.wait_recv()
-        weights = (weight_y[kind, 0], weight_y[kind, 1])
-        for pair in range(4):
-            lanes = pl.ds(pair * 128, 128)
-            values = jnp.concatenate([gather_y[chunk, k, :, lanes] for k in range(4)], axis=1)
-            out = contract3(split(values), weights, NN)
-            part_own[chunk, :, lanes] = out[:, :128]
-            part_send[chunk, :, lanes] = out[:, 128:]
+        ring_wait(2, chunk)
+        values = stacked(jnp.concatenate([in_y[chunk, k] for k in range(4)], axis=1))
+        for block in range(4):
+            lanes = pl.ds(block * 256, 256)
+            out = contract(values, weight_y[kind, 0, :, lanes], NN)
+            out = out[:128] + (out[128:] + contract(values[:128], weight_y[kind, 1, :, lanes], NN))
+            part_own[chunk, block] = out[:, :128]
+            part_send[chunk, block] = out[:, 128:]
         core_copy(chunk).start()
 
-    def step_back(chunk):
+    def step_e(chunk):
         core_copy(chunk).wait_recv()
+        turn_y[chunk] = part_own[chunk] + part_got[chunk]
+        ring_start(3, chunk)
+
+    def step_f(chunk):
+        ring_wait(3, chunk)
         for pair in range(4):
             for tile in range(4):
-                parts = []
-                for i in range(4):
-                    at = (chunk, pl.ds((tile * 4 + i) * 8, 8), pl.ds(pair * 128, 128))
-                    parts.append(part_own[at] + part_got[at])
-                parts = regroup(*parts)
+                parts = regroup(*[home_y[chunk, pair, pl.ds((tile * 4 + i) * 8, 8)] for i in range(4)])
                 for p in range(2):
                     for high in range(2):
                         rows = pl.ds(high * 256 + tile * 8 + pair * 2 + p, 8, stride=32)
@@ -204,10 +224,10 @@
     half[...] = jnp.exp(-0.05 * pot[...])
     values = split((half[...] * field[0]).reshape(512, 256))
     loads[2].wait()
-    step_z(0, split(lz[:128, :]), values)
+    step_z(0, stacked(lz[:128, :]), values)
     pl.semaphore_wait(barrier, 22)
     step_z_send(0)
-    step_z(1, split(lz[128:, :]), values)
+    step_z(1, stacked(lz[128:, :]), values)
     step_z_send(1)
 
     loads[3].wait()
@@ -223,55 +243,66 @@
     row = lax.broadcasted_iota(jnp.int32, (128, 256), 0)
     column = lax.broadcasted_iota(jnp.int32, (128, 256), 1)
     same = row // 64 == column % 128 // 64
-    at_x = pl.ds(pl.multiple_of(x * 128, 128), 128)
-    at_y = pl.ds(pl.multiple_of(y * 128, 128), 128)
     for kind in range(2):
         for k in range(4):
             block = pl.ds(k * 128, 128)
-            if kind == 0:
-                of_x, of_y = split(xy[at_x, block]), split(xy[at_y, block])
-            else:
-                of_x, of_y = split(xy[block, at_x]), split(xy[block, at_y])
+            parts = split(xy[block, :] if kind == 0 else xy[:, block])
+            columns = split(xy[:, block] if kind == 0 else xy[block, :])
             for part in range(2):
-                turned = contract(order_x, of_x[part], NN if kind == 0 else NT).astype(BF16)
-                weight_x[kind, part, :, block] = contract(turned, order_x, NT).astype(BF16)
-                turned = contract(order_y, of_y[part], NT if kind == 0 else NN).astype(BF16)
-                weight_y[kind, part, block, :] = jnp.where(same, contract(turned, order_out, NT), 0.0).astype(BF16)
+                rows = pl.ds(part * 512 + k * 128, 128)
+                turned = contract(order_x, parts[part], NN if kind == 0 else NT).astype(BF16)
+                for i in range(4):
+                    at = slice(i * 128, i * 128 + 128)
+                    weight_x[kind, rows, at] = contract(turned[:, at], order_x, NT).astype(BF16)
+                turned = contract(order_y, columns[part], NT if kind == 0 else NN).astype(BF16)
+                for i in range(4):
+                    value = contract(turned[:, i * 128 : i * 128 + 128], order_out, NT)
+                    weight_y[kind, part, block, pl.ds(i * 256, 256)] = jnp.where(same, value, 0.0).astype(BF16)
 
     turned = jnp.transpose(lz[...])
     values = split((half[...] * field[1]).reshape(512, 256))
-    step_z(2, split(turned[:128, :]), values)
-    step_z(3, split(turned[128:, :]), values)
-
-    step_x_send(0)
+    step_z(2, stacked(turned[:128, :]), values)
+    step_z(3, stacked(turned[128:, :]), values)
+
     step_z_send(2)
-    step_x_send(1)
     step_z_send(3)
-    step_y_send(0)
-    step_x_send(2)
-    step_y_send(1)
-    step_core_send(0)
-    step_x_send(3)
-    step_back(0)
-    step_y_send(2)
-    step_core_send(1)
-    step_back(1)
-    step_y_send(3)
-    step_core_send(2)
-    step_back(2)
-    step_core_send(3)
-    step_back(3)
-    for chunk in range(4):
+    step_a(0)
+    step_b(0)
+    step_c(0)
+    step_a(1)
+    step_d(0)
+    step_b(1)
+    step_e(0)
+    step_c(1)
+    step_f(0)
+    step_a(2)
+    step_d(1)
+    step_e(1)
+    step_b(2)
+    step_f(1)
+    step_c(2)
+    step_a(3)
+    step_d(2)
+    step_b(3)
+    step_e(2)
+    step_c(3)
+    step_f(2)
+    step_d(3)
+    step_e(3)
+    step_f(3)
+    for chunk in range(3):
         step_last(chunk)
 
     for chunk in range(4):
         wait_z_sent(send_z, z_send_sem, chunk)
-        wait_z_sent(send_back, b_send_sem, chunk)
-        for copy in ring_copies(gather_x, x_send_sem, x_recv_sem, chunk, 0):
-            copy.wait_send()
-        for copy in ring_copies(gather_y, y_send_sem, y_recv_sem, chunk, 1):
-            copy.wait_send()
+        for stage in range(4):
+            for copy in ring_copies(stage, chunk):
+                copy.wait_send()
         core_copy(chunk).wait_send()
+        if chunk < 3:
+            wait_z_sent(send_back, b_send_sem, chunk)
+    step_last(3)
+    wait_z_sent(send_back, b_send_sem, 3)
 
 
 def store(*refs):
@@ -290,9 +321,8 @@
 def body(start_field, end_adjoint, potential, line_xy, line_z):
     shape = start_field.shape
     dma = pltpu.SemaphoreType.DMA
-    chunk = (4, 128, 512)
     pieces = (4, 512, 128)
-    gather = (4, 4, 128, 512)
+    parts = (4, 4, 128, 128)
     outs = pl.pallas_call(
         kernel,
         out_shape=[jax.ShapeDtypeStruct(shape, F32)] * 3,
@@ -306,16 +336,12 @@
             pltpu.VMEM(line_z.shape, F32),
             pltpu.VMEM(pieces, F32),
             pltpu.VMEM(pieces, F32),
-            pltpu.VMEM(gather, F32),
-            pltpu.VMEM(gather, F32),
-            pltpu.VMEM(chunk, F32),
-            pltpu.VMEM(chunk, F32),
-            pltpu.VMEM(chunk, F32),
+            *[pltpu.VMEM(parts, F32)] * 10,
             pltpu.VMEM(pieces, F32),
             pltpu.VMEM(pieces, F32),
-            pltpu.VMEM((2, 2, 128, 512), BF16),
-            pltpu.VMEM((2, 2, 512, 256), BF16),
-            dma((5,)), dma((4,)), dma((4,)), dma((4, 3)), dma((4, 3)), dma((4, 3)), dma((4, 3)),
+            pltpu.VMEM((2, 1024, 512), BF16),
+            pltpu.VMEM((2, 2, 512, 1024), BF16),
+            dma((5,)), dma((4,)), dma((4,)), dma((4, 4, 3)), dma((4, 4, 3)),
             dma((4,)), dma((4,)), dma((4,)), dma((4,)),
         ],
         compiler_params=pltpu.CompilerParams(

time: 118 us -> 111 us (0.941)
  the two profiles are of different devices: /device:TPU:5 before, /device:TPU:1 now
where the time goes in v3:
time: 111 us
  Pallas kernels  110 us (99%)
    pallas_call x1, Pallas kernels, body(): pl.pallas_call(kernel, out_shape=[jax.ShapeDtypeStruct(shape, F32)] * 3,...  109 us

profile of v3, /device:TPU:1, one launch (start us, length us, event | category | flops | bytes accessed | tf_op | source)
XLA Modules:
  0.0 110.9 jit_solution(9781535096357543084)
XLA Ops:
  0.6 109.1 %contour_step.1 = (f32[16,32,256]{2,1,0:T(8,128)S(1)}, f32[16,32,256]{2,1,0:T(8,128)S(1)}, f32[16,32,256]{2,1,0:T(8,128)S(1)}) custom-call(f32[16,32,256]{2,1,0:T(8,128)} %start_hbm.1, f32[16,32,256]{2,1,0:T(8,128)} %end_hbm.1, f32[16,32,256]{2,1,0:T(8,128)} %potential_hbm.1, f32[512,512]{1,0:T(8,128)} %xy_hbm.1, f32[256,256]{1,0:T(8,128)} %z_hbm.1), custom_call_target="tpu_custom_call" | custom-call | tf_op jit(solution)/shard_map/contour_step/pallas_call | solution.py:326
  109.7 1.2 %store.1 = (f32[16,32,256]{2,1,0:T(8,128)}, f32[16,32,256]{2,1,0:T(8,128)}, f32[16,32,256]{2,1,0:T(8,128)}) custom-call(f32[16,32,256]{2,1,0:T(8,128)S(1)} %get-tuple-element.6.refs_0_, f32[16,32,256]{2,1,0:T(8,128)S(1)} %get-tuple-element.7.refs_1_, f32[16,32,256]{2,1,0:T(8,128)S(1)} %get-tuple-element.8.refs_2_), custom_call_target="tpu_custom_call" | custom-call | tf_op jit(solution)/shard_map/store/pallas_call | solution.py:352

commit v4 on v3

--- a/solution.py
+++ b/solution.py
@@ -59,8 +59,9 @@
             [(potential_hbm, pot), (start_hbm, field.at[0]), (z_hbm, lz), (xy_hbm, xy), (end_hbm, field.at[1])]
         )
     ]
-    for load in loads:
+    for load in loads[:3]:
         load.start()
+
     barrier = pltpu.get_barrier_semaphore()
 
     def signal(target):
@@ -75,19 +76,32 @@
         signal(device(x, (y + step) % 4, z, core))
     signal(device(x, y, z, 1 - core))
 
-    def exchange_z(source, target, send_sem, recv_sem, chunk):
+    def exchange_z(source, target, send_sem, recv_sem, chunk, first=0):
+        mine = pl.ds(pl.multiple_of(z * 32, 32), 32)
+
+        def send(peer):
+            pltpu.make_async_remote_copy(
+                source.at[chunk, pl.ds(pl.multiple_of(peer * 32, 32), 32)], target.at[chunk, mine],
+                send_sem.at[chunk], recv_sem.at[chunk],
+                device_id=device(x, y, peer, core), device_id_type=MESH,
+            ).start()
+
+        for peer in range(first):
+            @pl.when(peer != z)
+            def _(peer=peer):
+                send(peer)
+
         @pl.loop(0, NZ_CHIPS - 1)
         def _(i):
             step = NZ_CHIPS // 2 + i // 2 - (i % 2) * (2 * (i // 2) + 1)
             peer = (z + step) % NZ_CHIPS
-            pltpu.make_async_remote_copy(
-                source.at[chunk, pl.ds(pl.multiple_of(peer * 32, 32), 32)],
-                target.at[chunk, pl.ds(pl.multiple_of(z * 32, 32), 32)],
-                send_sem.at[chunk], recv_sem.at[chunk],
-                device_id=device(x, y, peer, core), device_id_type=MESH,
-            ).start()
-
-        mine = pl.ds(pl.multiple_of(z * 32, 32), 32)
+            if first == 0:
+                send(peer)
+            else:
+                @pl.when(peer >= first)
+                def _():
+                    send(peer)
+
         pltpu.make_async_copy(source.at[chunk, mine], target.at[chunk, mine], recv_sem.at[chunk]).start()
 
     def wait_z(target, recv_sem, chunk):
@@ -109,7 +123,7 @@
             copies.append(
                 pltpu.make_async_remote_copy(
                     source.at[chunk, there], target.at[chunk, here],
-                    ring_send_sem.at[stage, chunk, step - 1], ring_recv_sem.at[stage, chunk, step - 1],
+                    ring_send_sem.at[chunk], ring_recv_sem.at[stage, chunk],
                     device_id=peer, device_id_type=MESH,
                 )
             )
@@ -123,8 +137,8 @@
         target[chunk, here] = source[chunk, here]
 
     def ring_wait(stage, chunk):
-        for copy in ring_copies(stage, chunk):
-            copy.wait_recv()
+        got = exchanges[stage][1].at[chunk, pl.ds(0, 3)]
+        pltpu.make_async_copy(got, got, ring_recv_sem.at[stage, chunk]).wait()
 
     def core_copy(chunk):
         return pltpu.make_async_remote_copy(
@@ -201,7 +215,7 @@
                     for high in range(2):
                         rows = pl.ds(high * 256 + tile * 8 + pair * 2 + p, 8, stride=32)
                         send_back[chunk, rows, :] = parts[p * 2 + high]
-        exchange_z(send_back, got_back, b_send_sem, b_recv_sem, chunk)
+        exchange_z(send_back, got_back, b_send_sem, b_recv_sem, chunk, 8 if chunk == 3 else 0)
 
     def step_last(chunk):
         kind = chunk // 2
@@ -219,11 +233,12 @@
                 field[0, :, :, lanes] * value + final_out[:, :, lanes] * field[1, :, :, lanes]
             )
 
-    loads[0].wait()
-    loads[1].wait()
+    for load in loads[:3]:
+        load.wait()
+    for load in loads[3:]:
+        load.start()
     half[...] = jnp.exp(-0.05 * pot[...])
     values = split((half[...] * field[0]).reshape(512, 256))
-    loads[2].wait()
     step_z(0, stacked(lz[:128, :]), values)
     pl.semaphore_wait(barrier, 22)
     step_z_send(0)
@@ -295,9 +310,9 @@
 
     for chunk in range(4):
         wait_z_sent(send_z, z_send_sem, chunk)
-        for stage in range(4):
-            for copy in ring_copies(stage, chunk):
-                copy.wait_send()
+        for source in (out_x, turn_x, home_x, turn_y):
+            sent = source.at[chunk, pl.ds(0, 3)]
+            pltpu.make_async_copy(sent, sent, ring_send_sem.at[chunk]).wait()
         core_copy(chunk).wait_send()
         if chunk < 3:
             wait_z_sent(send_back, b_send_sem, chunk)
@@ -341,7 +356,7 @@
             pltpu.VMEM(pieces, F32),
             pltpu.VMEM((2, 1024, 512), BF16),
             pltpu.VMEM((2, 2, 512, 1024), BF16),
-            dma((5,)), dma((4,)), dma((4,)), dma((4, 4, 3)), dma((4, 4, 3)),
+            dma((5,)), dma((4,)), dma((4,)), dma((4,)), dma((4, 4)),
             dma((4,)), dma((4,)), dma((4,)), dma((4,)),
         ],
         compiler_params=pltpu.CompilerParams(

time: 111 us -> 106 us (0.955)
  the two profiles are of different devices: /device:TPU:1 before, /device:TPU:64 now
where the time goes in v4:
time: 106 us
  Pallas kernels  106 us (100%)
    pallas_call x1, Pallas kernels, body(): pl.pallas_call(kernel, out_shape=[jax.ShapeDtypeStruct(shape, F32)] * 3,...  104 us

profile of v4, /device:TPU:64, one launch (start us, length us, event | category | flops | bytes accessed | tf_op | source)
XLA Modules:
  0.0 106.3 jit_solution(12915615987371086959)
XLA Ops:
  0.6 104.5 %contour_step.1 = (f32[16,32,256]{2,1,0:T(8,128)S(1)}, f32[16,32,256]{2,1,0:T(8,128)S(1)}, f32[16,32,256]{2,1,0:T(8,128)S(1)}) custom-call(f32[16,32,256]{2,1,0:T(8,128)} %start_hbm.1, f32[16,32,256]{2,1,0:T(8,128)} %end_hbm.1, f32[16,32,256]{2,1,0:T(8,128)} %potential_hbm.1, f32[512,512]{1,0:T(8,128)} %xy_hbm.1, f32[256,256]{1,0:T(8,128)} %z_hbm.1), custom_call_target="tpu_custom_call" | custom-call | tf_op jit(solution)/shard_map/contour_step/pallas_call | solution.py:341
  105.1 1.2 %store.1 = (f32[16,32,256]{2,1,0:T(8,128)}, f32[16,32,256]{2,1,0:T(8,128)}, f32[16,32,256]{2,1,0:T(8,128)}) custom-call(f32[16,32,256]{2,1,0:T(8,128)S(1)} %get-tuple-element.6.refs_0_, f32[16,32,256]{2,1,0:T(8,128)S(1)} %get-tuple-element.7.refs_1_, f32[16,32,256]{2,1,0:T(8,128)S(1)} %get-tuple-element.8.refs_2_), custom_call_target="tpu_custom_call" | custom-call | tf_op jit(solution)/shard_map/store/pallas_call | solution.py:367

commit v5 on v4

--- a/solution.py
+++ b/solution.py
@@ -53,14 +53,20 @@
     def device(x_at, y_at, z_at, core_at):
         return {"px": x_at * 8 + z_at % 8, "py": y_at * 4 + (z_at // 8) * 2 + core_at}
 
-    loads = [
-        pltpu.make_async_copy(source, target, in_sem.at[i])
-        for i, (source, target) in enumerate(
-            [(potential_hbm, pot), (start_hbm, field.at[0]), (z_hbm, lz), (xy_hbm, xy), (end_hbm, field.at[1])]
-        )
-    ]
-    for load in loads[:3]:
-        load.start()
+    pairs = [(potential_hbm, pot), (start_hbm, field.at[0]), (z_hbm, lz), (xy_hbm, xy), (end_hbm, field.at[1])]
+
+    def load_start(i):
+        source, target = pairs[i]
+        rows = source.shape[0] // 4
+        for piece in range(4):
+            at = pl.ds(piece * rows, rows)
+            pltpu.make_async_copy(source.at[at], target.at[at], in_sem.at[i]).start()
+
+    def load_wait(i):
+        pltpu.make_async_copy(pairs[i][0], pairs[i][1], in_sem.at[i]).wait()
+
+    for i in range(3):
+        load_start(i)
 
     barrier = pltpu.get_barrier_semaphore()
 
@@ -233,10 +239,10 @@
                 field[0, :, :, lanes] * value + final_out[:, :, lanes] * field[1, :, :, lanes]
             )
 
-    for load in loads[:3]:
-        load.wait()
-    for load in loads[3:]:
-        load.start()
+    for i in range(3):
+        load_wait(i)
+    for i in range(3, 5):
+        load_start(i)
     half[...] = jnp.exp(-0.05 * pot[...])
     values = split((half[...] * field[0]).reshape(512, 256))
     step_z(0, stacked(lz[:128, :]), values)
@@ -245,8 +251,8 @@
     step_z(1, stacked(lz[128:, :]), values)
     step_z_send(1)
 
-    loads[3].wait()
-    loads[4].wait()
+    load_wait(3)
+    load_wait(4)
     row = lax.broadcasted_iota(jnp.int32, (128, 128), 0)
     column = lax.broadcasted_iota(jnp.int32, (128, 128), 1)
     order_x = (column == (row % 8) * 16 + row // 8).astype(F32).astype(BF16)
@@ -292,8 +298,8 @@
     step_f(0)
     step_a(2)
     step_d(1)
+    step_b(2)
     step_e(1)
-    step_b(2)
     step_f(1)
     step_c(2)
     step_a(3)
@@ -322,11 +328,12 @@
 
 def store(*refs):
     sources, targets, sem = refs[:3], refs[3:6], refs[6]
-    copies = [pltpu.make_async_copy(a, b, sem.at[i]) for i, (a, b) in enumerate(zip(sources, targets))]
-    for copy in copies:
-        copy.start()
-    for copy in copies:
-        copy.wait()
+    for i in range(3):
+        for piece in range(4):
+            at = pl.ds(piece * 4, 4)
+            pltpu.make_async_copy(sources[i].at[at], targets[i].at[at], sem.at[i]).start()
+    for i in range(3):
+        pltpu.make_async_copy(sources[i], targets[i], sem.at[i]).wait()
 
 
 def in_hbm(array):

time: 106 us -> 106 us (level)
  the two profiles are of different devices: /device:TPU:64 before, /device:TPU:128 now
where the time goes in v5:
time: 106 us
  Pallas kernels  106 us (100%)
    pallas_call x1, Pallas kernels, body(): pl.pallas_call(kernel, out_shape=[jax.ShapeDtypeStruct(shape, F32)] * 3,...  104 us

profile of v5, /device:TPU:128, one launch (start us, length us, event | category | flops | bytes accessed | tf_op | source)
XLA Modules:
  0.0 106.2 jit_solution(11105269960650116749)
XLA Ops:
  0.6 104.5 %contour_step.1 = (f32[16,32,256]{2,1,0:T(8,128)S(1)}, f32[16,32,256]{2,1,0:T(8,128)S(1)}, f32[16,32,256]{2,1,0:T(8,128)S(1)}) custom-call(f32[16,32,256]{2,1,0:T(8,128)} %start_hbm.1, f32[16,32,256]{2,1,0:T(8,128)} %end_hbm.1, f32[16,32,256]{2,1,0:T(8,128)} %potential_hbm.1, f32[512,512]{1,0:T(8,128)} %xy_hbm.1, f32[256,256]{1,0:T(8,128)} %z_hbm.1), custom_call_target="tpu_custom_call" | custom-call | tf_op jit(solution)/shard_map/contour_step/pallas_call | solution.py:348
  105.1 1.2 %store.1 = (f32[16,32,256]{2,1,0:T(8,128)}, f32[16,32,256]{2,1,0:T(8,128)}, f32[16,32,256]{2,1,0:T(8,128)}) custom-call(f32[16,32,256]{2,1,0:T(8,128)S(1)} %get-tuple-element.6.refs_0_, f32[16,32,256]{2,1,0:T(8,128)S(1)} %get-tuple-element.7.refs_1_, f32[16,32,256]{2,1,0:T(8,128)S(1)} %get-tuple-element.8.refs_2_), custom_call_target="tpu_custom_call" | custom-call | tf_op jit(solution)/shard_map/store/pallas_call | solution.py:374
